TPU v7x, 512 devices: a whole 4x8x8 slice. The times are simulated.
512 devices in a mesh: row: 8 (over x, core), col: 16 (over y_lo, z), layer: 4 (over y_hi).
Axes of the slice: x: 4, y: 8 (y_hi: 4, y_lo: 2; y = y_hi * 2 + y_lo), z: 8, core: 2. Of those that a mesh axis runs over, the one named last changes fastest.
Arguments:
- hamiltonian: bfloat16 [8192, 8192], P('row', ('col', 'layer')), as said below
- inv_root: bfloat16 [8192, 8192], P('row', 'col'), as said below
- h_pattern: int32 [32, 32], replicated, may hold values from 0 to 1, as said below
- z_pattern: int32 [32, 32], replicated, may hold values from 0 to 1, as said below
Outputs:
- transformed: bfloat16 [8192, 8192], P('row', ('col', 'layer'))
Inputs may be any that keep to these rules, and one draw needn't show every extreme that they name: hamiltonian is symmetric. inv_root is symmetric. h_pattern is symmetric and every diagonal block is present. z_pattern is symmetric and every diagonal block is present.
All inputs are finite; a program needn't handle non-finite values.
Results may differ from a plain program's by a relative error of at most 0.005.
Values may be sent and summed in bfloat16 or wider, within the bound.
A program may use at most 64 MiB of HBM per device.

v0:
```python
import jax
import jax.numpy as jnp
from jax import lax
from jax.sharding import PartitionSpec as P

BS = 256


def mask_tile(tile, pattern, row_start, col_start):
    blocks = pattern.shape[0]
    block_ids = jnp.arange(blocks, dtype=jnp.int32)
    row_ids = (row_start + jnp.arange(tile.shape[0], dtype=jnp.int32)) // BS
    col_ids = (col_start + jnp.arange(tile.shape[1], dtype=jnp.int32)) // BS
    row_pick = (row_ids[:, None] == block_ids[None, :]).astype(jnp.float32)
    col_pick = (block_ids[:, None] == col_ids[None, :]).astype(jnp.float32)
    inner = jnp.dot(pattern.astype(jnp.float32), col_pick, precision=lax.Precision.HIGHEST)
    keep = jnp.dot(row_pick, inner, precision=lax.Precision.HIGHEST)
    return jnp.where(keep > 0.5, tile, jnp.zeros_like(tile))


def accumulate(left, right):
    return jnp.dot(left, right, preferred_element_type=jnp.float32)


def local(hamiltonian, inv_root, h_pattern, z_pattern):
    rows_here = inv_root.shape[0]
    cols_here = inv_root.shape[1]
    quarter = hamiltonian.shape[1]
    layers = lax.axis_size("layer")
    per_row = lax.axis_size("col") // lax.axis_size("row")
    row_index = lax.axis_index("row")
    col_index = lax.axis_index("col")
    layer_index = lax.axis_index("layer")
    h_local = mask_tile(
        hamiltonian, h_pattern, row_index * rows_here, col_index * cols_here + layer_index * quarter
    )
    z_local = mask_tile(inv_root, z_pattern, row_index * rows_here, col_index * cols_here)
    h_whole = lax.all_gather(h_local, "col", axis=1, tiled=True)
    z_layered = z_local.reshape(per_row, layers, quarter, cols_here)
    z_part = lax.dynamic_index_in_dim(z_layered, layer_index, 1, keepdims=False).reshape(
        per_row * quarter, cols_here
    )
    columns = h_whole
    partial_y = accumulate(columns, lax.all_gather(z_part, "row", axis=0, tiled=True))
    z_quarter = lax.dynamic_slice_in_dim(z_local, layer_index * quarter, quarter, 1)
    z_rows = lax.all_gather(z_quarter, "col", axis=1, tiled=True)
    summed = lax.psum(partial_y, "layer")
    layered = summed.reshape(per_row, layers, quarter, cols_here)
    own_rows = lax.dynamic_index_in_dim(layered, layer_index, 1, keepdims=False).reshape(
        per_row * quarter, cols_here
    )
    y_own = own_rows.astype(jnp.bfloat16)
    columns = z_rows
    partial_c = accumulate(columns, lax.all_gather(y_own, "row", axis=0, tiled=True))
    result = lax.psum_scatter(partial_c, "layer", scatter_dimension=1, tiled=True)
    return result.astype(jnp.bfloat16)


def solution(mesh):
    return jax.shard_map(
        local,
        mesh=mesh,
        in_specs=(P("row", ("col", "layer")), P("row", "col"), P(), P()),
        out_specs=P("row", ("col", "layer")),
        check_vma=False,
    )
```

profile of v0, /device:TPU:20, one launch (start us, length us, event | category | flops | bytes accessed | tf_op | source)
XLA Modules:
  0.0 365.5 jit_solution(18108361089963021768)
XLA Ops:
  6.5 0.0 copy-start
  6.5 0.0 copy-start.1
  6.5 0.0 all-gather.9.cloned.1.call-start
  6.6 1.1 fusion.4
  7.7 2.3 compare_select_fusion
  10.0 0.7 constant_dynamic-slice_fusion
  10.7 0.0 all-gather.9.cloned.1.call-update
  10.7 0.0 all-gather.7.cloned.1.call-start
  10.8 0.0 copy-done
  10.8 0.2 fusion.7
  11.1 0.0 copy-done.1
  11.1 1.2 fusion
  12.2 0.0 all-gather.7.cloned.1.call-update
  12.3 0.0 all-gather.5.cloned.1.call-start
  12.3 0.7 constant_dynamic-slice_fusion.1
  13.1 0.0 all-gather.5.cloned.1.call-update
  13.1 0.0 all-gather.11.cloned.1.call-start
  13.1 31.7 %all-gather.9.cloned.1.call-done = bf16[2048,512]{1,0:T(8,128)(2,1)} async-done(((bf16[256,512]{1,0:T(8,128)(2,1)}), bf16[2048,512]{1,0:T(8,128)(2,1)}) %all-gather.9.cloned.1.call-update) | async-done | bytes 2097168 | tf_op jit(solution)/shard_map/all_gather | solution.py:44
  44.9 95.0 %all-gather.7.cloned.1.call-done = bf16[1024,2048]{1,0:T(8,128)(2,1)} async-done(((bf16[1024,128]{1,0:T(8,128)(2,1)}), bf16[1024,2048]{1,0:T(8,128)(2,1)}) %all-gather.7.cloned.1.call-update) | async-done | bytes 4194320 | tf_op jit(solution)/shard_map/all_gather | solution.py:38
  139.8 5.2 %fusion.19 = f32[1024,512]{1,0:T(8,128)S(1)} fusion(bf16[1024,2048]{1,0:T(8,128)(2,1)} %all-gather.7.cloned.1.call-done, bf16[2048,512]{1,0:T(8,128)(2,1)} %all-gather.9.cloned.1.call-done), kind=kOutput, calls=%fused_computation.41 | convolution fusion | flops 2147483648 | bytes 8388608 | tf_op jit(solution)/shard_map/dot_general | solution.py:22
  145.0 90.8 %all-reduce.1 = bf16[2,4,128,512]{3,2,1,0:T(8,128)(2,1)S(1)} all-reduce(f32[2,4,128,512]{3,2,1,0:T(8,128)S(1)} %bitcast.10), channel_id=1, replica_groups=mesh['row'=8,'col'=16,'layer'=4] {'layer'}, use_global_device_ids=true, to_apply=%region_0.1 | all-reduce | flops 524288 | bytes 3145728 | tf_op jit(solution)/shard_map/psum | solution.py:47
  235.8 0.7 dynamic-slice_convert_fusion
  236.6 0.0 all-gather.11.cloned.1.call-update
  236.6 0.0 reduce-scatter.2.cloned.1.call-start
  236.6 30.9 %all-gather.5.cloned.1.call-done = bf16[1024,2048]{1,0:T(8,128)(2,1)} async-done(((bf16[1024,128]{1,0:T(8,128)(2,1)}), bf16[1024,2048]{1,0:T(8,128)(2,1)}) %all-gather.5.cloned.1.call-update) | async-done | bytes 4194320 | tf_op jit(solution)/shard_map/all_gather | solution.py:46
  267.5 28.2 %all-gather.11.cloned.1.call-done = bf16[2048,512]{1,0:T(8,128)(2,1)} async-done(((bf16[256,512]{1,0:T(8,128)(2,1)}), bf16[2048,512]{1,0:T(8,128)(2,1)}) %all-gather.11.cloned.1.call-update) | async-done | bytes 2097168 | tf_op jit(solution)/shard_map/all_gather | solution.py:54
  295.6 6.5 %fusion.20 = f32[1024,512]{1,0:T(8,128)} fusion(bf16[1024,2048]{1,0:T(8,128)(2,1)} %all-gather.5.cloned.1.call-done, bf16[2048,512]{1,0:T(8,128)(2,1)} %all-gather.11.cloned.1.call-done), kind=kOutput, calls=%fused_computation.42 | convolution fusion | flops 2147483648 | bytes 8388608 | tf_op jit(solution)/shard_map/dot_general | solution.py:22
  302.2 0.0 reduce-scatter.2.cloned.1.call-update
  302.2 55.0 %reduce-scatter.2.cloned.1.call-done = f32[1024,128]{1,0:T(8,128)} async-done(((f32[1024,512]{1,0:T(8,128)}), f32[1024,128]{1,0:T(8,128)}) %reduce-scatter.2.cloned.1.call-update) | async-done | bytes 524304 | tf_op jit(solution)/shard_map/reduce_scatter | solution.py:55
  357.2 1.8 convert_element_type.23
  (3 shorter events, 0.0 us)
Async XLA Ops:
  6.5 4.3 %copy-start = (s32[32,32]{1,0:T(8,128)S(1)}, s32[32,32]{1,0:T(8,128)}, u32[]{:S(2)}) copy-start(s32[32,32]{1,0:T(8,128)} %param.6) | copy-start | bytes 12292
  6.5 4.5 %copy-start.1 = (bf16[1024,128]{1,0:T(8,128)(2,1)S(1)}, bf16[1024,128]{1,0:T(8,128)(2,1)}, u32[]{:S(2)}) copy-start(bf16[1024,128]{1,0:T(8,128)(2,1)} %param.4) | copy-start | bytes 786436
  6.5 38.3 %all-gather.9.cloned.1.call-start = ((), (), s32[]{:S(2)}) async-start(), calls=%async_computation.3 | async-start | bytes 2359296 | tf_op jit(solution)/shard_map/all_gather | solution.py:44
  10.7 129.1 %all-gather.7.cloned.1.call-start = ((), (), s32[]{:S(2)}) async-start(), calls=%async_computation.2 | async-start | bytes 4456448 | tf_op jit(solution)/shard_map/all_gather | solution.py:38
  12.3 255.2 %all-gather.5.cloned.1.call-start = ((), (), s32[]{:S(2)}) async-start(), calls=%async_computation.1 | async-start | bytes 4456448 | tf_op jit(solution)/shard_map/all_gather | solution.py:46
  13.1 282.6 %all-gather.11.cloned.1.call-start = ((), (), s32[]{:S(2)}) async-start(), calls=%async_computation.4 | async-start | bytes 2359296 | tf_op jit(solution)/shard_map/all_gather | solution.py:54
  236.6 120.7 %reduce-scatter.2.cloned.1.call-start = ((), (), s32[]{:S(2)}) async-start(), calls=%async_computation.5 | async-start | bytes 2621440 | tf_op jit(solution)/shard_map/reduce_scatter | solution.py:55
Sparse Core Ops, SparseCore 0:
  10.9 33.9 all-gather.8
  46.9 92.9 all-gather.6
  141.9 125.5 all-gather.4
  269.5 26.1 all-gather.10
  302.3 54.8 reduce-scatter.1
where the time goes:
time: 366 us
  waiting for transfers between devices  241 us (66%)
  blocking collectives  90.8 us (25%)
  matrix products  16.5 us (5%)
  between operations  13.2 us (4%)
    all_gather x1, waiting for transfers between devices, local(): h_whole = lax.all_gather(h_local, 'col', axis=1, tiled=True)  95 us
    psum x1, blocking collectives, local(): summed = lax.psum(partial_y, 'layer')  90.8 us
    reduce_scatter x1, waiting for transfers between devices, local(): lax.psum_scatter(partial_c, 'layer', scatter_dimension=1, tiled=True)  55 us
    all_gather x1, waiting for transfers between devices, local(): lax.all_gather(z_part, 'row', axis=0, tiled=True)  31.7 us
    all_gather x1, waiting for transfers between devices, local(): z_rows = lax.all_gather(z_quarter, 'col', axis=1, tiled=True)  30.9 us
    all_gather x1, waiting for transfers between devices, local(): lax.all_gather(y_own, 'row', axis=0, tiled=True)  28.2 us
    dot_general x2, matrix products, accumulate(): return jnp.dot(left, right, preferred_element_type=jnp.float32)  11.7 us
  transfers between devices with their start and end apart: 5, of which 5 were waited for; matrix products, arithmetic and copies ran while one was open for 2% of the time, Pallas kernels for 0%

commit v1 on v0

--- a/solution.py
+++ b/solution.py
@@ -23,6 +23,22 @@
 
 
 def local(hamiltonian, inv_root, h_pattern, z_pattern):
+
+    def serve_side_now(k_dim, arr, mesh_name):
+        p_count = lax.axis_size(mesh_name)
+        all_rows = [(i0, (i0 + 1) % p_count) for i0 in range(p_count)]
+        formed, low = ([arr], [arr])
+        blocks_here = [(i0, (i0 - 1) % p_count) for i0 in range(p_count)]
+        for _ in range(p_count // 2):
+            formed.append(lax.ppermute(formed[-1], axis_name=mesh_name, perm=all_rows))
+        for _ in range((p_count - 1) // 2):
+            low.append(lax.ppermute(low[-1], axis_name=mesh_name, perm=blocks_here))
+        return jnp.roll(
+            jnp.concatenate([*formed[::-1], *low[1:]], k_dim),
+            (lax.axis_index(mesh_name) - p_count // 2) * arr.shape[k_dim],
+            k_dim,
+        )
+
     rows_here = inv_root.shape[0]
     cols_here = inv_root.shape[1]
     quarter = hamiltonian.shape[1]
@@ -41,7 +57,7 @@
         per_row * quarter, cols_here
     )
     columns = h_whole
-    partial_y = accumulate(columns, lax.all_gather(z_part, "row", axis=0, tiled=True))
+    partial_y = accumulate(columns, serve_side_now(0, z_part, "row"))
     z_quarter = lax.dynamic_slice_in_dim(z_local, layer_index * quarter, quarter, 1)
     z_rows = lax.all_gather(z_quarter, "col", axis=1, tiled=True)
     summed = lax.psum(partial_y, "layer")

time: 366 us -> 334 us (0.913)
  waiting for transfers between devices: 241 us -> 191 us
  local copies, waits for them, and re-layouts: 2.21 us -> 13.1 us
  starting transfers between devices: 0.17 us -> 5.78 us
    all_gather x1, waiting for transfers between devices: 95 us -> 57.1 us  [local(): h_whole = lax.all_gather(h_local, 'col', axis=1, tiled=True)]
    all_gather x1 -> x0, waiting for transfers between devices: 31.7 us -> none  [local(): lax.all_gather(z_part, 'row', axis=0, tiled=True)]
    ppermute x0 -> x7, waiting for transfers between devices: none -> 17.5 us  [the longest x4 17.5 us: serve_side_now(): formed.append(lax.ppermute(formed[-1], axis_name=mesh_name, perm=all_rows))]
    unnamed x4 -> x15, local copies, waits for them, and re-layouts: 0.01 us -> 10.9 us
    ppermute x0 -> x7, starting transfers between devices: none -> 5.65 us  [the longest x3 5.63 us: serve_side_now(): low.append(lax.ppermute(low[-1], axis_name=mesh_name, perm=blocks_here))]
  transfers between devices with their start and end apart: 5 -> 11, of which waited for: 5 -> 8; matrix products, arithmetic and copies ran while one was open for 2% -> 6% of each run, Pallas kernels for 0% -> 0%
where the time goes in v1:
time: 334 us; the launch traced here: 333 us
  waiting for transfers between devices  191 us (57%)
  blocking collectives  90.5 us (27%)
  matrix products  18.1 us (5%)
  between operations  13.2 us (4%)
  local copies, waits for them, and re-layouts  13.1 us (4%)
  starting transfers between devices  5.78 us (2%)
    psum x1, blocking collectives, local(): summed = lax.psum(partial_y, 'layer')  90.5 us
    all_gather x1, waiting for transfers between devices, local(): h_whole = lax.all_gather(h_local, 'col', axis=1, tiled=True)  57.1 us
    reduce_scatter x1, waiting for transfers between devices, local(): lax.psum_scatter(partial_c, 'layer', scatter_dimension=1, tiled=True)  55 us
    all_gather x1, waiting for transfers between devices, local(): z_rows = lax.all_gather(z_quarter, 'col', axis=1, tiled=True)  31.3 us
    all_gather x1, waiting for transfers between devices, local(): lax.all_gather(y_own, 'row', axis=0, tiled=True)  29.8 us
    ppermute x4, waiting for transfers between devices, serve_side_now(): formed.append(lax.ppermute(formed[-1], axis_name=mesh_name, perm=all_rows))  17.5 us
    dot_general x2, matrix products, accumulate(): return jnp.dot(left, right, preferred_element_type=jnp.float32)  11.7 us
    unnamed x15, local copies, waits for them, and re-layouts  10.9 us
  transfers between devices with their start and end apart: 11, of which 8 were waited for; matrix products, arithmetic and copies ran while one was open for 6% of the time, Pallas kernels for 0%

profile of v1, /device:TPU:20, one launch (start us, length us, event | category | flops | bytes accessed | tf_op | source)
XLA Modules:
  0.0 333.3 jit_solution(18170141652305973481)
XLA Ops:
  6.6 1.0 fusion.9
  7.5 2.1 fusion.2
  9.7 0.0 all-gather.6.cloned.1.call-update
  9.7 0.0 all-gather.4.cloned.1.call-start
  9.8 1.0 fusion.6
  10.8 2.3 compare_select_fusion
  13.1 0.7 constant_dynamic-slice_fusion.1
  13.9 0.0 all-gather.4.cloned.1.call-update
  13.9 0.0 all-gather.8.cloned.1.call-start
  14.0 0.0 collective-permute-start
  14.0 5.8 %collective-permute-done = bf16[256,512]{1,0:T(8,128)(2,1)S(1)} collective-permute-done((bf16[256,512]{1,0:T(8,128)(2,1)S(1)}, bf16[256,512]{1,0:T(8,128)(2,1)S(1)}, u32[]{:S(2)}, u32[]{:S(2)}) %collective-permute-start) | collective-permute-done | bytes 262176 | tf_op jit(solution)/shard_map/ppermute | solution.py:33
  19.8 1.7 collective-permute-start.4
  21.5 4.1 %collective-permute-done.1 = bf16[256,512]{1,0:T(8,128)(2,1)S(1)} collective-permute-done((bf16[256,512]{1,0:T(8,128)(2,1)S(1)}, bf16[256,512]{1,0:T(8,128)(2,1)S(1)}, u32[]{:S(2)}, u32[]{:S(2)}) %collective-permute-start.1) | collective-permute-done | bytes 262176 | tf_op jit(solution)/shard_map/ppermute | solution.py:33
  25.6 0.0 collective-permute-done.4
  25.6 1.7 collective-permute-start.5
  27.3 4.0 %collective-permute-done.2 = bf16[256,512]{1,0:T(8,128)(2,1)S(1)} collective-permute-done((bf16[256,512]{1,0:T(8,128)(2,1)S(1)}, bf16[256,512]{1,0:T(8,128)(2,1)S(1)}, u32[]{:S(2)}, u32[]{:S(2)}) %collective-permute-start.2) | collective-permute-done | bytes 262176 | tf_op jit(solution)/shard_map/ppermute | solution.py:33
  31.4 0.0 collective-permute-start.3
  31.4 0.0 collective-permute-done.5
  31.4 2.1 collective-permute-start.6
  33.5 3.6 %collective-permute-done.3 = bf16[256,512]{1,0:T(8,128)(2,1)S(1)} collective-permute-done((bf16[256,512]{1,0:T(8,128)(2,1)S(1)}, bf16[256,512]{1,0:T(8,128)(2,1)S(1)}, u32[]{:S(2)}, u32[]{:S(2)}) %collective-permute-start.3) | collective-permute-done | bytes 262176 | tf_op jit(solution)/shard_map/ppermute | solution.py:33
  37.2 0.7 constant_dynamic-update-slice_fusion.15
  37.9 0.7 constant_dynamic-update-slice_fusion.14
  38.7 0.7 constant_dynamic-update-slice_fusion.13
  39.4 0.7 constant_dynamic-update-slice_fusion.12
  40.1 0.7 constant_dynamic-update-slice_fusion.11
  40.9 0.7 constant_dynamic-update-slice_fusion.10
  41.6 0.7 constant_dynamic-update-slice_fusion.9
  42.3 0.7 constant_dynamic-update-slice_fusion.8
  43.0 0.7 constant_dynamic-update-slice_fusion.7
  43.8 0.7 constant_dynamic-update-slice_fusion.6
  44.5 0.7 constant_dynamic-update-slice_fusion.5
  45.2 0.7 constant_dynamic-update-slice_fusion.4
  45.9 0.7 constant_dynamic-update-slice_fusion.3
  46.6 0.7 constant_dynamic-update-slice_fusion.2
  47.4 0.7 constant_dynamic-update-slice_fusion.1
  48.1 0.7 constant_dynamic-update-slice_fusion
  48.8 57.1 %all-gather.6.cloned.1.call-done = bf16[1024,2048]{1,0:T(8,128)(2,1)} async-done(((bf16[1024,128]{1,0:T(8,128)(2,1)}), bf16[1024,2048]{1,0:T(8,128)(2,1)}) %all-gather.6.cloned.1.call-update) | async-done | bytes 4194320 | tf_op jit(solution)/shard_map/all_gather | solution.py:54
  105.9 5.2 %fusion = f32[1024,512]{1,0:T(8,128)S(1)} fusion(bf16[1024,2048]{1,0:T(8,128)(2,1)} %all-gather.6.cloned.1.call-done, bf16[4096,512]{1,0:T(8,128)(2,1)} %constant_dynamic-update-slice_fusion, s32[]{:T(128)S(6)} %select_n.66), kind=kOutput, calls=%fused_computation | convolution fusion | flops 2147483648 | bytes 8388612 | tf_op jit(solution)/shard_map/dot_general | solution.py:22
  111.1 90.5 %all-reduce.1 = bf16[2,4,128,512]{3,2,1,0:T(8,128)(2,1)S(1)} all-reduce(f32[2,4,128,512]{3,2,1,0:T(8,128)S(1)} %bitcast.13), channel_id=1, replica_groups=mesh['row'=8,'col'=16,'layer'=4] {'layer'}, use_global_device_ids=true, to_apply=%region_0.1 | all-reduce | flops 524288 | bytes 3145728 | tf_op jit(solution)/shard_map/psum | solution.py:63
  201.6 0.7 dynamic-slice_convert_fusion
  202.3 0.0 all-gather.8.cloned.1.call-update
  202.3 0.0 reduce-scatter.2.cloned.1.call-start
  202.4 31.3 %all-gather.4.cloned.1.call-done = bf16[1024,2048]{1,0:T(8,128)(2,1)} async-done(((bf16[1024,128]{1,0:T(8,128)(2,1)}), bf16[1024,2048]{1,0:T(8,128)(2,1)}) %all-gather.4.cloned.1.call-update) | async-done | bytes 4194320 | tf_op jit(solution)/shard_map/all_gather | solution.py:62
  233.7 29.8 %all-gather.8.cloned.1.call-done = bf16[2048,512]{1,0:T(8,128)(2,1)} async-done(((bf16[256,512]{1,0:T(8,128)(2,1)}), bf16[2048,512]{1,0:T(8,128)(2,1)}) %all-gather.8.cloned.1.call-update) | async-done | bytes 2097168 | tf_op jit(solution)/shard_map/all_gather | solution.py:70
  263.4 6.5 %fusion.22 = f32[1024,512]{1,0:T(8,128)} fusion(bf16[1024,2048]{1,0:T(8,128)(2,1)} %all-gather.4.cloned.1.call-done, bf16[2048,512]{1,0:T(8,128)(2,1)} %all-gather.8.cloned.1.call-done), kind=kOutput, calls=%fused_computation.60 | convolution fusion | flops 2147483648 | bytes 8388608 | tf_op jit(solution)/shard_map/dot_general | solution.py:22
  270.0 0.0 reduce-scatter.2.cloned.1.call-update
  270.0 55.0 %reduce-scatter.2.cloned.1.call-done = f32[1024,128]{1,0:T(8,128)} async-done(((f32[1024,512]{1,0:T(8,128)}), f32[1024,128]{1,0:T(8,128)}) %reduce-scatter.2.cloned.1.call-update) | async-done | bytes 524304 | tf_op jit(solution)/shard_map/reduce_scatter | solution.py:71
  325.0 1.8 convert_element_type.23
  (8 shorter events, 0.1 us)
Async XLA Ops:
  6.5 99.4 %all-gather.6.cloned.1.call-start = ((), (), s32[]{:S(2)}) async-start(), calls=%async_computation.2 | async-start | bytes 4456448 | tf_op jit(solution)/shard_map/all_gather | solution.py:54
  9.7 224.0 %all-gather.4.cloned.1.call-start = ((), (), s32[]{:S(2)}) async-start(), calls=%async_computation.1 | async-start | bytes 4456448 | tf_op jit(solution)/shard_map/all_gather | solution.py:62
  13.9 249.5 %all-gather.8.cloned.1.call-start = ((), (), s32[]{:S(2)}) async-start(), calls=%async_computation.3 | async-start | bytes 2359296 | tf_op jit(solution)/shard_map/all_gather | solution.py:70
  14.0 5.8 %collective-permute-start = (bf16[256,512]{1,0:T(8,128)(2,1)S(1)}, bf16[256,512]{1,0:T(8,128)(2,1)S(1)}, u32[]{:S(2)}, u32[]{:S(2)}) collective-permute-start(bf16[256,512]{1,0:T(8,128)(2,1)S(1)} %bitcast.9), channel_id=1, source_target_pairs={{0,64},{64,128},{128,192},{192,256},{256,320},{320,384},{384,448},... | collective-permute-start | bytes 786440 | tf_op jit(solution)/shard_map/ppermute | solution.py:33
  19.8 5.8 %collective-permute-start.1 = (bf16[256,512]{1,0:T(8,128)(2,1)S(1)}, bf16[256,512]{1,0:T(8,128)(2,1)S(1)}, u32[]{:S(2)}, u32[]{:S(2)}) collective-permute-start(bf16[256,512]{1,0:T(8,128)(2,1)S(1)} %collective-permute-done), channel_id=1, source_target_pairs={{0,64},{64,128},{128,192},{192,256},{256,320},{320,384},{384,448},... | collective-permute-start | bytes 786440 | tf_op jit(solution)/shard_map/ppermute | solution.py:33
  19.8 5.8 %collective-permute-start.4 = (bf16[256,512]{1,0:T(8,128)(2,1)S(1)}, bf16[256,512]{1,0:T(8,128)(2,1)S(1)}, u32[]{:S(2)}, u32[]{:S(2)}) collective-permute-start(bf16[256,512]{1,0:T(8,128)(2,1)S(1)} %bitcast.10), channel_id=1, source_target_pairs={{0,448},{64,0},{128,64},{192,128},{256,192},{320,256},{384,320},{4... | collective-permute-start | bytes 786440 | tf_op jit(solution)/shard_map/ppermute | solution.py:35
  25.6 5.8 %collective-permute-start.2 = (bf16[256,512]{1,0:T(8,128)(2,1)S(1)}, bf16[256,512]{1,0:T(8,128)(2,1)S(1)}, u32[]{:S(2)}, u32[]{:S(2)}) collective-permute-start(bf16[256,512]{1,0:T(8,128)(2,1)S(1)} %collective-permute-done.1), channel_id=1, source_target_pairs={{0,64},{64,128},{128,192},{192,256},{256,320},{320,384},{384,448},... | collective-permute-start | bytes 786440 | tf_op jit(solution)/shard_map/ppermute | solution.py:33
  25.6 5.8 %collective-permute-start.5 = (bf16[256,512]{1,0:T(8,128)(2,1)S(1)}, bf16[256,512]{1,0:T(8,128)(2,1)S(1)}, u32[]{:S(2)}, u32[]{:S(2)}) collective-permute-start(bf16[256,512]{1,0:T(8,128)(2,1)S(1)} %collective-permute-done.4), channel_id=1, source_target_pairs={{0,448},{64,0},{128,64},{192,128},{256,192},{320,256},{384,320},{4... | collective-permute-start | bytes 786440 | tf_op jit(solution)/shard_map/ppermute | solution.py:35
  31.4 5.8 %collective-permute-start.3 = (bf16[256,512]{1,0:T(8,128)(2,1)S(1)}, bf16[256,512]{1,0:T(8,128)(2,1)S(1)}, u32[]{:S(2)}, u32[]{:S(2)}) collective-permute-start(bf16[256,512]{1,0:T(8,128)(2,1)S(1)} %collective-permute-done.2), channel_id=1, source_target_pairs={{0,64},{64,128},{128,192},{192,256},{256,320},{320,384},{384,448},... | collective-permute-start | bytes 786440 | tf_op jit(solution)/shard_map/ppermute | solution.py:33
  31.4 10.9 %collective-permute-start.6 = (bf16[256,512]{1,0:T(8,128)(2,1)S(1)}, bf16[256,512]{1,0:T(8,128)(2,1)S(1)}, u32[]{:S(2)}, u32[]{:S(2)}) collective-permute-start(bf16[256,512]{1,0:T(8,128)(2,1)S(1)} %collective-permute-done.5), channel_id=1, source_target_pairs={{0,448},{64,0},{128,64},{192,128},{256,192},{320,256},{384,320},{4... | collective-permute-start | bytes 786440 | tf_op jit(solution)/shard_map/ppermute | solution.py:35
  202.3 122.7 %reduce-scatter.2.cloned.1.call-start = ((), (), s32[]{:S(2)}) async-start(), calls=%async_computation.4 | async-start | bytes 2621440 | tf_op jit(solution)/shard_map/reduce_scatter | solution.py:71
Sparse Core Ops, SparseCore 0:
  9.8 96.0 all-gather.5
  107.9 125.7 all-gather.3
  235.8 27.5 all-gather.7
  270.1 54.8 reduce-scatter.1
